TPU v7x, 256 devices: a whole 4x4x8 slice. The times are simulated.
256 devices in a mesh: row: 32 (over z_lo, x, core), col: 8 (over y, z_hi).
Axes of the slice: x: 4, y: 4, z: 8 (z_hi: 2, z_lo: 4; z = z_hi * 4 + z_lo), core: 2. Of those that a mesh axis runs over, the one named last changes fastest.
Arguments:
- amplitudes: bfloat16 [1536, 65536], P('row', 'col'), may hold values from -6 to 6
- integrals: bfloat16 [2048, 65536], P(None, ('col', 'row')), may hold values from -0.09375 to 0.09375
- residual_in: float32 [1536, 2048], P('row', 'col'), may hold values from -6 to 6
Outputs:
- residual_out: float32 [1536, 2048], P('row', 'col')
All inputs are finite; a program needn't handle non-finite values.
Results may differ from a plain program's by a relative error of at most 0.0003.
Values may be sent and summed in bfloat16 or wider, within the bound.
A program may use at most 64 MiB of HBM per device.

v0:
```python
import jax
import jax.numpy as jnp
from jax import lax
from jax.sharding import PartitionSpec as P


def local(amplitudes, integrals, residual_in):
    regrouped = lax.all_to_all(amplitudes, "row", split_axis=1, concat_axis=0, tiled=True)
    row_count = lax.axis_size("row")
    col_count = lax.axis_size("col")
    unit_length = regrouped.shape[1]
    left_block = regrouped.reshape(row_count, -1, unit_length)
    right_block = integrals.reshape(col_count, -1, unit_length)
    partial_value = jnp.einsum(
        "rmk,cnk->rcmn", left_block, right_block, preferred_element_type=jnp.float32
    )
    partial_value = partial_value.reshape(-1, right_block.shape[1])
    ladder = lax.psum_scatter(partial_value, ("row", "col"), scatter_dimension=0, tiled=True)
    return residual_in + ladder


def solution(mesh):
    return jax.shard_map(
        local,
        mesh=mesh,
        in_specs=(P("row", "col"), P(None, ("col", "row")), P("row", "col")),
        out_specs=P("row", "col"),
        check_vma=False,
    )
```

profile of v0, /device:TPU:32, one launch (start us, length us, event | category | flops | bytes accessed | tf_op | source)
XLA Modules:
  0.0 1601.3 jit_solution(15672727377036626955)
XLA Ops:
  6.5 0.0 copy-start
  6.5 0.0 reduce-scatter.2.cloned.1.call-start
  6.5 1.3 copy.9
  7.8 28.9 %all_to_all.16 = bf16[48,32,256]{2,0,1:T(8,128)(2,1)S(1)} all-to-all(bf16[48,32,256]{2,0,1:T(8,128)(2,1)S(1)} %bitcast.20), channel_id=1, replica_groups=mesh['row'=32,'col'=8] {'row'}, dimensions={1} | all-to-all | bytes 1572864 | tf_op jit(solution)/shard_map/all_to_all | solution.py:8
  36.7 0.0 copy-done
  36.7 6.3 convolution_bitcast_fusion
  43.0 11.0 copy.5
  54.0 0.0 copy-start.1
  54.0 0.0 reduce-scatter.2.cloned.1.call-update
  54.0 1539.0 %reduce-scatter.2.cloned.1.call-done = f32[48,256]{1,0:T(8,128)} async-done(((f32[12288,256]{1,0:T(8,128)}), f32[48,256]{1,0:T(8,128)}) %reduce-scatter.2.cloned.1.call-update) | async-done | bytes 49168 | tf_op jit(solution)/shard_map/reduce_scatter | solution.py:18
  1593.0 0.0 copy-done.1
  1593.0 1.4 add.5
Async XLA Ops:
  6.5 30.1 %copy-start = (bf16[2048,256]{1,0:T(8,128)(2,1)S(1)}, bf16[2048,256]{1,0:T(8,128)(2,1)}, u32[]{:S(2)}) copy-start(bf16[2048,256]{1,0:T(8,128)(2,1)} %param.4) | copy-start | bytes 3145732
  6.5 1586.5 %reduce-scatter.2.cloned.1.call-start = ((), (), s32[]{:S(2)}) async-start(), calls=%async_computation.2 | async-start | bytes 12632064 | tf_op jit(solution)/shard_map/reduce_scatter | solution.py:18
  54.0 1539.1 %copy-start.1 = (f32[48,256]{1,0:T(8,128)S(1)}, f32[48,256]{1,0:T(8,128)}, u32[]{:S(2)}) copy-start(f32[48,256]{1,0:T(8,128)} %param.5) | copy-start | bytes 147460
Sparse Core Ops, SparseCore 0:
  54.1 1538.8 reduce-scatter.1
where the time goes:
time: 1600 us
  waiting for transfers between devices  1540 us (96%)
  blocking collectives  28.9 us (2%)
    reduce_scatter x1, waiting for transfers between devices, local(): lax.psum_scatter(partial_value, ('row', 'col'), scatter_dimension=0, tile...  1540 us
  transfers between devices with their start and end apart: 1, of which 1 were waited for; matrix products, arithmetic and copies ran while one was open for 0% of the time, Pallas kernels for 0%

commit v1 on v0

v1 whole, which is shorter than its diff:
```python
import functools

import jax
import jax.numpy as jnp
from jax import lax
from jax.experimental import pallas as pl
from jax.experimental.pallas import tpu as pltpu
from jax.sharding import PartitionSpec as P

MESH = pl.DeviceIdType.MESH
ROWS = 48
COLS = 256
UNIT = 256
DEPTH = 4 * UNIT
BLOCKS = 8
OFFSETS = (2, 1, 3, 0)
TOP = (0, 4, 3, 6)
BOTTOM = (2, 1, 5, 7)


def device(x, y, z, core):
    x, y, z = lax.rem(x + 4, 4), lax.rem(y + 4, 4), lax.rem(z + 8, 8)
    return (lax.rem(z, 4) * 8 + x * 2 + core, y * 2 + lax.div(z, 4))


def kernel(
    a_ref, b_ref, out_ref,
    a_all, b_all, part, near, far, z_first, z_ring, z_last, x_last,
    a_send, a_recv, b_local, mate_send, mate_recv, bx_send, bx_recv, fw_send, fw_recv,
    near_send, near_recv, far_send, far_recv, zf_send, zf_recv, zr_send, zr_recv, zl_send, zl_recv, xl_send, xl_recv,
):
    row, col = lax.axis_index("row"), lax.axis_index("col")
    core = lax.rem(row, 2)
    x = lax.rem(lax.div(row, 2), 4)
    z_low = lax.div(row, 8)
    y = lax.div(col, 2)
    z_high = lax.rem(col, 2)
    z = z_high * 4 + z_low
    mate = device(x, y, z, 1 - core)
    toward = 1 - 2 * core
    way = 1 - lax.rem(z_low, 2)
    sign = 1 - 2 * way

    z_lows = (z_low, z_low + 1 - 2 * lax.rem(z_low, 2), 3 - z_low, lax.rem(z_low + 2, 4))

    barrier = pltpu.get_barrier_semaphore()
    partners = [mate, device(x + 1, y, z, core), device(x - 1, y, z, core)]
    partners += [device(x, y + 1, z, core), device(x, y - 1, z, core)]
    partners += [device(x + dx, y, z + dz, core) for dx in (0, 2) for dz in (1, -1)]
    partners += [device(x + dx, y, z_high * 4 + low, core) for low in z_lows for dx in (0, 2)][1:]
    for partner in partners:
        pl.semaphore_signal(barrier, inc=1, device_id=partner, device_id_type=MESH)

    def unit(start):
        return pl.ds(pl.multiple_of(start * UNIT, UNIT), UNIT)

    def a_pieces(dx, low):
        there = lax.rem(x + dx, 4)
        block = a_all.at[z_low, pl.ds(ROWS * (dx // 2), ROWS)]
        for units, slot, length in (
            (low * 8 + there * 2, 0, 2),
            (low * 8 + lax.rem(there + 3, 4) * 2, 2, 1),
            (low * 8 + lax.rem(there + 1, 4) * 2 + 1, 3, 1),
        ):
            source = a_ref.at[:, pl.ds(pl.multiple_of(units * UNIT, UNIT), length * UNIT)]
            yield source, block.at[:, slot * UNIT : (slot + length) * UNIT]

    def a_start(dx, turn):
        low = z_lows[turn]
        for source, target in a_pieces(dx, low):
            if dx == 0 and turn == 0:
                pltpu.make_async_copy(source, target, a_recv.at[0, 0]).start()
            else:
                pltpu.make_async_remote_copy(
                    source, target, a_send.at[turn, dx // 2], a_recv.at[turn, dx // 2],
                    device_id=device(x + dx, y, z_high * 4 + low, core), device_id_type=MESH,
                ).start()

    def a_copy(dx, turn):
        block = a_all.at[z_lows[turn], pl.ds(ROWS * (dx // 2), ROWS)]
        if dx == 0 and turn == 0:
            return pltpu.make_async_copy(block, block, a_recv.at[0, 0])
        return pltpu.make_async_remote_copy(
            block, block, a_send.at[turn, dx // 2], a_recv.at[turn, dx // 2], device_id=mate, device_id_type=MESH
        )

    def b_place(half, i):
        high = 1 - z_high if half == 0 else z_high
        return high, lax.rem(y + OFFSETS[i], 4)

    def b_across(half, i):
        high, ys = b_place(half, i)
        return pltpu.make_async_remote_copy(
            b_ref.at[ys, high], b_all.at[high, ys, :, unit(2 + core)], bx_send.at[half, i], bx_recv.at[half, i],
            device_id=device(x + toward, y, z, core), device_id_type=MESH,
        )

    def b_forward(half, i, slot):
        high, ys = b_place(half, i)
        here = b_all.at[high, ys, :, unit(slot)]
        return pltpu.make_async_remote_copy(
            here, here, fw_send.at[half, i], fw_recv.at[half, i], device_id=mate, device_id_type=MESH
        )

    def b_own(half):
        high = 1 - z_high if half == 0 else z_high
        return pltpu.make_async_copy(b_ref.at[:, high], b_all.at[high, :, :, unit(core)], b_local.at[half])

    def b_mate(half, slot):
        high = 1 - z_high if half == 0 else z_high
        return pltpu.make_async_remote_copy(
            b_ref.at[:, high], b_all.at[high, :, :, unit(slot)], mate_send.at[half], mate_recv.at[half],
            device_id=mate, device_id_type=MESH,
        )

    a_start(0, 0)
    b_own(0).start()
    b_own(1).start()
    pl.semaphore_wait(barrier, len(partners))
    for i in range(4):
        b_across(0, i).start()
    b_mate(0, core).start()
    a_start(2, 0)
    for turn in (1, 2):
        for dx in (0, 2):
            a_start(dx, turn)
    for i in range(4):
        b_across(1, i).start()
    b_mate(1, core).start()
    for dx in (0, 2):
        a_start(dx, 3)

    steps = (4, 3 * sign, -3 * sign, 2 * sign, -2 * sign, sign, -sign, 0)
    turns = (0, 1, 2, 3, 3, 2, 1, 0)

    def multiply(b, i):
        to = lax.rem(z + steps[b] + 8, 8)
        ys = lax.rem(y + OFFSETS[i], 4)
        product = lax.dot_general(
            a_all[lax.rem(to, 4)], b_all[lax.div(to, 4), ys], (((1,), (1,)), ((), ())), preferred_element_type=jnp.float32
        )
        part[b, TOP[i]] = product[:ROWS]
        part[b, BOTTOM[i]] = product[ROWS:]

    def near_copy(b, d):
        return pltpu.make_async_remote_copy(
            part.at[b, pl.ds(2 * d, 2)], near.at[b, d], near_send.at[b, d], near_recv.at[b, d],
            device_id=device(x, y + 1 - 2 * d, z, core), device_id_type=MESH,
        )

    def far_copy(b, d):
        return pltpu.make_async_remote_copy(
            part.at[b, 4 + d], far.at[b, d], far_send.at[b, d], far_recv.at[b, d],
            device_id=device(x, y + 1 - 2 * d, z, core), device_id_type=MESH,
        )

    def z_first_copy(d):
        return pltpu.make_async_remote_copy(
            part.at[0, 6 + d], z_first.at[d], zf_send.at[d], zf_recv.at[d],
            device_id=device(x, y, z + 1 - 2 * d, core), device_id_type=MESH,
        )

    def z_ring_copy(b, d, step):
        return pltpu.make_async_remote_copy(
            part.at[b, pl.ds(6, 2)], z_ring.at[step, d], zr_send.at[step, d], zr_recv.at[step, d],
            device_id=device(x, y, z + 1 - 2 * d, core), device_id_type=MESH,
        )

    def z_last_copy(b, d, half):
        return pltpu.make_async_remote_copy(
            part.at[b, 6 + half], z_last.at[half, d], zl_send.at[half, d], zl_recv.at[half, d],
            device_id=device(x + 2 * half, y, z + 1 - 2 * d, core), device_id_type=MESH,
        )

    x_last_copy = pltpu.make_async_remote_copy(
        part.at[7, 7], x_last, xl_send, xl_recv, device_id=device(x + 2, y, z, core), device_id_type=MESH
    )

    def begin(b):
        turn = turns[b]
        if b < 4:
            for dx in (0, 2):
                if dx == 0 and turn == 0:
                    a_copy(0, 0).wait()
                else:
                    a_copy(dx, turn).wait_recv()
        half = {0: 0, 2: 1}.get(b)
        if half is not None:
            b_own(half).wait()
            b_mate(half, 1 - core).wait_recv()
        for i in range(4):
            if half is not None:
                b_across(half, i).wait_recv()
                b_forward(half, i, 2 + core).start()
                b_forward(half, i, 3 - core).wait_recv()
            multiply(b, i)
            if i in (1, 2):
                near_copy(b, i - 1).start()

    def pass_on(b):
        for d in range(2):
            near_copy(b, d).wait_recv()
            part[b, 4 + d] += near[b, d, 0]
            far_copy(b, d).start()

    def finish(b):
        for d in range(2):
            far_copy(b, d).wait_recv()
        part[b, 6] += far[b, 0] + near[b, 1, 1]
        part[b, 7] += far[b, 1] + near[b, 0, 1]
        d = way if b % 2 else 1 - way
        if b == 0:
            z_first_copy(0).start()
            z_first_copy(1).start()
        elif b < 3:
            z_first_copy(d).wait_recv()
            part[b, 6 + d] += z_first[d]
            z_ring_copy(b, d, 0).start()
        elif b < 7:
            step = (b - 3) // 2
            z_ring_copy(b, d, step).wait_recv()
            part[b, pl.ds(6, 2)] += z_ring[step, d]
            if step == 0:
                z_ring_copy(b, d, 1).start()
            else:
                z_last_copy(b, d, 1).start()
                z_last_copy(b, d, 0).start()
        else:
            x_last_copy.start()

    for t in range(BLOCKS + 2):
        if t < BLOCKS:
            begin(t)
        if 0 <= t - 1 < BLOCKS:
            pass_on(t - 1)
        if 0 <= t - 2:
            finish(t - 2)

    for half in range(2):
        for d in range(2):
            z_last_copy(5, d, half).wait_recv()
    x_last_copy.wait_recv()
    out_ref[...] = part[7, 6] + x_last[...] + z_last[0, 0] + z_last[0, 1] + z_last[1, 0] + z_last[1, 1]

    for turn in range(4):
        for dx in (0, 2):
            if turn or dx:
                a_copy(dx, turn).wait_send()
    for half in range(2):
        b_mate(half, core).wait_send()
        for i in range(4):
            b_across(half, i).wait_send()
            b_forward(half, i, 2 + core).wait_send()
    for b in range(BLOCKS):
        for d in range(2):
            near_copy(b, d).wait_send()
            far_copy(b, d).wait_send()
    for d in range(2):
        z_first_copy(d).wait_send()
        for step in range(2):
            z_ring_copy(1, d, step).wait_send()
        for half in range(2):
            z_last_copy(5, d, half).wait_send()
    x_last_copy.wait_send()


def local(amplitudes, integrals, residual_in):
    pieces = integrals.reshape(4, 2, COLS, UNIT)
    dma = pltpu.SemaphoreType.DMA
    ladder = pl.pallas_call(
        kernel,
        out_shape=jax.ShapeDtypeStruct((ROWS, COLS), jnp.float32),
        in_specs=[pl.BlockSpec(memory_space=pl.ANY)] * 2,
        out_specs=pl.BlockSpec(memory_space=pltpu.VMEM),
        scratch_shapes=[
            pltpu.VMEM((4, 2 * ROWS, DEPTH), jnp.bfloat16),
            pltpu.VMEM((2, 4, COLS, DEPTH), jnp.bfloat16),
            pltpu.VMEM((BLOCKS, 8, ROWS, COLS), jnp.float32),
            pltpu.VMEM((BLOCKS, 2, 2, ROWS, COLS), jnp.float32),
            pltpu.VMEM((BLOCKS, 2, ROWS, COLS), jnp.float32),
            pltpu.VMEM((2, ROWS, COLS), jnp.float32),
            pltpu.VMEM((2, 2, 2, ROWS, COLS), jnp.float32),
            pltpu.VMEM((2, 2, ROWS, COLS), jnp.float32),
            pltpu.VMEM((ROWS, COLS), jnp.float32),
            dma((4, 2)), dma((4, 2)), dma((2,)), dma((2,)), dma((2,)), dma((2, 4)), dma((2, 4)), dma((2, 4)), dma((2, 4)),
            dma((BLOCKS, 2)), dma((BLOCKS, 2)), dma((BLOCKS, 2)), dma((BLOCKS, 2)),
            dma((2,)), dma((2,)), dma((2, 2)), dma((2, 2)), dma((2, 2)), dma((2, 2)), dma(()), dma(()),
        ],
        compiler_params=pltpu.CompilerParams(collective_id=0, has_side_effects=True, vmem_limit_bytes=40 << 20),
        name="ladder",
    )(amplitudes, pieces)
    return residual_in + ladder


def solution(mesh):
    return jax.shard_map(
        local,
        mesh=mesh,
        in_specs=(P("row", "col"), P(None, ("col", "row")), P("row", "col")),
        out_specs=P("row", "col"),
        check_vma=False,
    )
```

time: 1600 us -> 68.1 us (0.04)
  waiting for transfers between devices: 1540 us -> 0 us
  Pallas kernels: 0 us -> 64.2 us
  blocking collectives: 28.9 us -> 0 us
    reduce_scatter x1 -> x0, waiting for transfers between devices: 1540 us -> none  [local(): lax.psum_scatter(partial_value, ('row', 'col'), scatter_dimension=0, tile...]
    pallas_call x0 -> x1, Pallas kernels: none -> 64.2 us  [local(): pl.pallas_call(kernel, out_shape=jax.ShapeDtypeStruct((ROWS, COLS), jnp.f...]
    all_to_all x1 -> x0, blocking collectives: 28.9 us -> none  [local(): lax.all_to_all(amplitudes, 'row', split_axis=1, concat_axis=0, tiled=True)]
  transfers between devices with their start and end apart: 1 -> 0, of which waited for: 1 -> 0; matrix products, arithmetic and copies ran while one was open for 0% -> 0% of each run, Pallas kernels for 0% -> 0%
where the time goes in v1:
time: 68.1 us; the launch traced here: 67.2 us
  Pallas kernels  64.2 us (94%)
  local copies, waits for them, and re-layouts  2.36 us (3%)
    pallas_call x1, Pallas kernels, local(): pl.pallas_call(kernel, out_shape=jax.ShapeDtypeStruct((ROWS, COLS), jnp.f...  64.2 us
    unnamed x6, local copies, waits for them, and re-layouts  2.36 us

profile of v1, /device:TPU:32, one launch (start us, length us, event | category | flops | bytes accessed | tf_op | source)
XLA Modules:
  0.0 67.2 jit_solution(15381565243743731785)
XLA Ops:
  0.0 0.0 copy-start
  0.0 1.2 %copy-done = bf16[2048,256]{1,0:T(8,128)(2,1)S(1)} copy-done((bf16[2048,256]{1,0:T(8,128)(2,1)S(1)}, bf16[2048,256]{1,0:T(8,128)(2,1)}, u32[]{:S(2)}) %copy-start) | copy-done | bytes 1048600
  1.2 0.0 copy-start.1
  1.2 1.1 %copy-done.1 = bf16[48,8192]{1,0:T(8,128)(2,1)S(1)} copy-done((bf16[48,8192]{1,0:T(8,128)(2,1)S(1)}, bf16[48,8192]{1,0:T(8,128)(2,1)}, u32[]{:S(2)}) %copy-start.1) | copy-done | bytes 786456
  2.4 0.0 copy-start.2
  2.4 64.2 %ladder.1 = f32[48,256]{1,0:T(8,128)S(1)} custom-call(bf16[48,8192]{1,0:T(8,128)(2,1)S(1)} %copy-done.1, bf16[4,2,256,256]{3,2,1,0:T(8,128)(2,1)S(1)} %bitcast.1), custom_call_target="tpu_custom_call" | custom-call | tf_op jit(solution)/shard_map/ladder/pallas_call | solution.py:270
  66.6 0.0 copy-done.2
  66.6 0.6 add.3
Async XLA Ops:
  0.0 1.2 %copy-start = (bf16[2048,256]{1,0:T(8,128)(2,1)S(1)}, bf16[2048,256]{1,0:T(8,128)(2,1)}, u32[]{:S(2)}) copy-start(bf16[2048,256]{1,0:T(8,128)(2,1)} %param.4) | copy-start | bytes 3145732
  1.2 1.1 %copy-start.1 = (bf16[48,8192]{1,0:T(8,128)(2,1)S(1)}, bf16[48,8192]{1,0:T(8,128)(2,1)}, u32[]{:S(2)}) copy-start(bf16[48,8192]{1,0:T(8,128)(2,1)} %a_ref.1) | copy-start | bytes 2359300
  2.4 64.2 %copy-start.2 = (f32[48,256]{1,0:T(8,128)S(1)}, f32[48,256]{1,0:T(8,128)}, u32[]{:S(2)}) copy-start(f32[48,256]{1,0:T(8,128)} %param.5) | copy-start | bytes 147460

commit v2 on v1

--- a/solution.py
+++ b/solution.py
@@ -13,9 +13,20 @@
 UNIT = 256
 DEPTH = 4 * UNIT
 BLOCKS = 8
+EARLY = 1
 OFFSETS = (2, 1, 3, 0)
 TOP = (0, 4, 3, 6)
 BOTTOM = (2, 1, 5, 7)
+
+OUTER = (4, 3, 0, -1, -3, 2, -2, 1)
+INNER = (4, 3, 0, -1, -3, -2, 2, 1)
+OUTER_TURNS = (2, 4, 4, 10, 6, 8, 8, 9)
+INNER_TURNS = (2, 4, 4, 10, 6, 7, 8, 10)
+SCHEDULE = {
+    "init": [("b", 0, 0), ("b", 0, 1), ("m", 0), ("a", 2, 0), ("a", 0, 1), ("b", 0, 2), ("b", 0, 3), ("a", 2, 1),
+             ("b", 1, 0), ("b", 1, 1), ("b", 1, 2), ("b", 1, 3), ("a", 0, 2), ("a", 0, 3), ("a", 2, 2), ("a", 2, 3)],
+    ("end", 0): [("m", 1)],
+}
 
 
 def device(x, y, z, core):
@@ -40,6 +51,7 @@
     toward = 1 - 2 * core
     way = 1 - lax.rem(z_low, 2)
     sign = 1 - 2 * way
+    outer = 1 - lax.rem(lax.div(z_low + 1, 2), 2)
 
     z_lows = (z_low, z_low + 1 - 2 * lax.rem(z_low, 2), 3 - z_low, lax.rem(z_low + 2, 4))
 
@@ -113,25 +125,22 @@
             device_id=mate, device_id_type=MESH,
         )
 
+    def run(when):
+        for op in SCHEDULE.get(when, ()):
+            if op[0] == "b":
+                b_across(op[1], op[2]).start()
+            elif op[0] == "m":
+                b_mate(op[1], core).start()
+            else:
+                a_start(op[1], op[2])
+
     a_start(0, 0)
     b_own(0).start()
     b_own(1).start()
     pl.semaphore_wait(barrier, len(partners))
-    for i in range(4):
-        b_across(0, i).start()
-    b_mate(0, core).start()
-    a_start(2, 0)
-    for turn in (1, 2):
-        for dx in (0, 2):
-            a_start(dx, turn)
-    for i in range(4):
-        b_across(1, i).start()
-    b_mate(1, core).start()
-    for dx in (0, 2):
-        a_start(dx, 3)
-
-    steps = (4, 3 * sign, -3 * sign, 2 * sign, -2 * sign, sign, -sign, 0)
-    turns = (0, 1, 2, 3, 3, 2, 1, 0)
+    run("init")
+
+    steps = [sign * (step_out * outer + step_in * (1 - outer)) for step_out, step_in in zip(OUTER, INNER, strict=True)]
 
     def multiply(b, i):
         to = lax.rem(z + steps[b] + 8, 8)
@@ -173,29 +182,36 @@
         )
 
     x_last_copy = pltpu.make_async_remote_copy(
-        part.at[7, 7], x_last, xl_send, xl_recv, device_id=device(x + 2, y, z, core), device_id_type=MESH
+        part.at[2, 7], x_last, xl_send, xl_recv, device_id=device(x + 2, y, z, core), device_id_type=MESH
     )
 
+    def forward(half, i):
+        b_across(half, i).wait_recv()
+        b_forward(half, i, 2 + core).start()
+        run(("got", half, i))
+
     def begin(b):
-        turn = turns[b]
-        if b < 4:
-            for dx in (0, 2):
-                if dx == 0 and turn == 0:
-                    a_copy(0, 0).wait()
-                else:
-                    a_copy(dx, turn).wait_recv()
+        turn = {0: 0, 1: 1, 4: 2, 5: 3}.get(b)
+        if turn == 0:
+            a_copy(0, 0).wait()
+            a_copy(2, 0).wait_recv()
+        elif turn is not None:
+            a_copy(0, turn).wait_recv()
+            a_copy(2, turn).wait_recv()
+
         half = {0: 0, 2: 1}.get(b)
         if half is not None:
             b_own(half).wait()
             b_mate(half, 1 - core).wait_recv()
         for i in range(4):
             if half is not None:
-                b_across(half, i).wait_recv()
-                b_forward(half, i, 2 + core).start()
+                if b == 0 or i >= EARLY:
+                    forward(half, i)
                 b_forward(half, i, 3 - core).wait_recv()
             multiply(b, i)
             if i in (1, 2):
                 near_copy(b, i - 1).start()
+        run(("end", b))
 
     def pass_on(b):
         for d in range(2):
@@ -208,19 +224,19 @@
             far_copy(b, d).wait_recv()
         part[b, 6] += far[b, 0] + near[b, 1, 1]
         part[b, 7] += far[b, 1] + near[b, 0, 1]
-        d = way if b % 2 else 1 - way
-        if b == 0:
+    def along_z(b, step):
+        d = way if step > 0 else 1 - way
+        if step == 4:
             z_first_copy(0).start()
             z_first_copy(1).start()
-        elif b < 3:
+        elif abs(step) == 3:
             z_first_copy(d).wait_recv()
             part[b, 6 + d] += z_first[d]
             z_ring_copy(b, d, 0).start()
-        elif b < 7:
-            step = (b - 3) // 2
-            z_ring_copy(b, d, step).wait_recv()
-            part[b, pl.ds(6, 2)] += z_ring[step, d]
-            if step == 0:
+        elif step:
+            z_ring_copy(b, d, 2 - abs(step)).wait_recv()
+            part[b, pl.ds(6, 2)] += z_ring[2 - abs(step), d]
+            if abs(step) == 2:
                 z_ring_copy(b, d, 1).start()
             else:
                 z_last_copy(b, d, 1).start()
@@ -228,19 +244,29 @@
         else:
             x_last_copy.start()
 
-    for t in range(BLOCKS + 2):
+    def move(t, steps, turns):
+        for b in sorted(range(BLOCKS), key=lambda b: (-abs(steps[b]), b)):
+            if turns[b] == t:
+                along_z(b, steps[b])
+
+    for t in range(max(OUTER_TURNS + INNER_TURNS) + 1):
         if t < BLOCKS:
             begin(t)
         if 0 <= t - 1 < BLOCKS:
             pass_on(t - 1)
-        if 0 <= t - 2:
+        if t == 1:
+            for i in range(EARLY):
+                forward(1, i)
+        if 0 <= t - 2 < BLOCKS:
             finish(t - 2)
+        pl.when(outer == 1)(functools.partial(move, t, OUTER, OUTER_TURNS))
+        pl.when(outer == 0)(functools.partial(move, t, INNER, INNER_TURNS))
 
     for half in range(2):
         for d in range(2):
             z_last_copy(5, d, half).wait_recv()
     x_last_copy.wait_recv()
-    out_ref[...] = part[7, 6] + x_last[...] + z_last[0, 0] + z_last[0, 1] + z_last[1, 0] + z_last[1, 1]
+    out_ref[...] = part[2, 6] + x_last[...] + z_last[0, 0] + z_last[0, 1] + z_last[1, 0] + z_last[1, 1]
 
     for turn in range(4):
         for dx in (0, 2):
@@ -286,7 +312,7 @@
             dma((BLOCKS, 2)), dma((BLOCKS, 2)), dma((BLOCKS, 2)), dma((BLOCKS, 2)),
             dma((2,)), dma((2,)), dma((2, 2)), dma((2, 2)), dma((2, 2)), dma((2, 2)), dma(()), dma(()),
         ],
-        compiler_params=pltpu.CompilerParams(collective_id=0, has_side_effects=True, vmem_limit_bytes=40 << 20),
+        compiler_params=pltpu.CompilerParams(collective_id=0, has_side_effects=True, vmem_limit_bytes=60 << 20),
         name="ladder",
     )(amplitudes, pieces)
     return residual_in + ladder

time: 68.1 us -> 65.4 us (0.960); the launches traced: 67.2 us -> 65.2 us
  local copies, waits for them, and re-layouts: 2.36 us -> 0.01 us
  other arithmetic: 0.63 us -> 1.43 us
    unnamed x6 -> x2, local copies, waits for them, and re-layouts: 2.36 us -> 0.01 us
    add x1, other arithmetic: 0.63 us -> 1.43 us  [local(): return residual_in + ladder]
where the time goes in v2:
time: 65.4 us; the launch traced here: 65.2 us
  Pallas kernels  63.8 us (98%)
  other arithmetic  1.43 us (2%)
    pallas_call x1, Pallas kernels, local(): pl.pallas_call(kernel, out_shape=jax.ShapeDtypeStruct((ROWS, COLS), jnp.f...  63.8 us
    add x1, other arithmetic, local(): return residual_in + ladder  1.43 us

profile of v2, /device:TPU:32, one launch (start us, length us, event | category | flops | bytes accessed | tf_op | source)
XLA Modules:
  0.0 65.2 jit_solution(8721580038727166882)
XLA Ops:
  0.0 0.0 copy-start
  0.0 63.8 %ladder.1 = f32[48,256]{1,0:T(8,128)} custom-call(bf16[48,8192]{1,0:T(8,128)(2,1)} %a_ref.1, bf16[4,2,256,256]{3,2,1,0:T(8,128)(2,1)} %bitcast.1), custom_call_target="tpu_custom_call" | custom-call | tf_op jit(solution)/shard_map/ladder/pallas_call | solution.py:296
  63.8 0.0 copy-done
  63.8 1.4 %add.3 = f32[48,256]{1,0:T(8,128)} add(f32[48,256]{1,0:T(8,128)S(1)} %copy-done, f32[48,256]{1,0:T(8,128)} %ladder.1) | non-fusion elementwise | flops 12288 | bytes 147456 | tf_op jit(solution)/shard_map/add | solution.py:318
Async XLA Ops:
  0.0 63.8 %copy-start = (f32[48,256]{1,0:T(8,128)S(1)}, f32[48,256]{1,0:T(8,128)}, u32[]{:S(2)}) copy-start(f32[48,256]{1,0:T(8,128)} %param.5) | copy-start | bytes 147460

commit v3 on v2

--- a/solution.py
+++ b/solution.py
@@ -13,7 +13,6 @@
 UNIT = 256
 DEPTH = 4 * UNIT
 BLOCKS = 8
-EARLY = 1
 OFFSETS = (2, 1, 3, 0)
 TOP = (0, 4, 3, 6)
 BOTTOM = (2, 1, 5, 7)
@@ -23,9 +22,10 @@
 OUTER_TURNS = (2, 4, 4, 10, 6, 8, 8, 9)
 INNER_TURNS = (2, 4, 4, 10, 6, 7, 8, 10)
 SCHEDULE = {
-    "init": [("b", 0, 0), ("b", 0, 1), ("m", 0), ("a", 2, 0), ("a", 0, 1), ("b", 0, 2), ("b", 0, 3), ("a", 2, 1),
-             ("b", 1, 0), ("b", 1, 1), ("b", 1, 2), ("b", 1, 3), ("a", 0, 2), ("a", 0, 3), ("a", 2, 2), ("a", 2, 3)],
-    ("end", 0): [("m", 1)],
+    "init": [("b", 0, 0), ("m", 0), ("a", 2, 0), ("a", 0, 1), ("b", 0, 1), ("a", 2, 1), ("b", 0, 2), ("b", 0, 3), ("a", 0, 2), ("a", 0, 3)],
+    ("got", 0, 0): [("b", 1, 0), ("b", 1, 1), ("b", 1, 2), ("b", 1, 3)],
+    ("got", 0, 3): [("m", 1), ("a", 2, 2)],
+    ("got", 1, 0): [("a", 2, 3)],
 }
 
 
@@ -151,9 +151,9 @@
         part[b, TOP[i]] = product[:ROWS]
         part[b, BOTTOM[i]] = product[ROWS:]
 
-    def near_copy(b, d):
-        return pltpu.make_async_remote_copy(
-            part.at[b, pl.ds(2 * d, 2)], near.at[b, d], near_send.at[b, d], near_recv.at[b, d],
+    def near_copy(b, d, place):
+        return pltpu.make_async_remote_copy(
+            part.at[b, 2 * d + place], near.at[b, d, place], near_send.at[b, d, place], near_recv.at[b, d, place],
             device_id=device(x, y + 1 - 2 * d, z, core), device_id_type=MESH,
         )
 
@@ -190,38 +190,42 @@
         b_forward(half, i, 2 + core).start()
         run(("got", half, i))
 
-    def begin(b):
-        turn = {0: 0, 1: 1, 4: 2, 5: 3}.get(b)
-        if turn == 0:
+    def chunk(b, i):
+        multiply(b, i)
+        if i == 0:
+            near_copy(b, 0, 0).start()
+            near_copy(b, 1, 0).start()
+        elif i < 3:
+            near_copy(b, i - 1, 1).start()
+
+    def got_a(turn):
+        if turn:
+            a_copy(0, turn).wait_recv()
+        else:
             a_copy(0, 0).wait()
-            a_copy(2, 0).wait_recv()
-        elif turn is not None:
-            a_copy(0, turn).wait_recv()
-            a_copy(2, turn).wait_recv()
-
-        half = {0: 0, 2: 1}.get(b)
-        if half is not None:
+        a_copy(2, turn).wait_recv()
+
+    def got_b(half, i):
+        if i == 0:
             b_own(half).wait()
             b_mate(half, 1 - core).wait_recv()
+        forward(half, i)
+        b_forward(half, i, 3 - core).wait_recv()
+
+    def begin(b):
         for i in range(4):
-            if half is not None:
-                if b == 0 or i >= EARLY:
-                    forward(half, i)
-                b_forward(half, i, 3 - core).wait_recv()
-            multiply(b, i)
-            if i in (1, 2):
-                near_copy(b, i - 1).start()
-        run(("end", b))
+            chunk(b, i)
 
     def pass_on(b):
         for d in range(2):
-            near_copy(b, d).wait_recv()
+            near_copy(b, d, 0).wait_recv()
             part[b, 4 + d] += near[b, d, 0]
             far_copy(b, d).start()
 
     def finish(b):
         for d in range(2):
             far_copy(b, d).wait_recv()
+            near_copy(b, d, 1).wait_recv()
         part[b, 6] += far[b, 0] + near[b, 1, 1]
         part[b, 7] += far[b, 1] + near[b, 0, 1]
     def along_z(b, step):
@@ -249,18 +253,55 @@
             if turns[b] == t:
                 along_z(b, steps[b])
 
-    for t in range(max(OUTER_TURNS + INNER_TURNS) + 1):
-        if t < BLOCKS:
-            begin(t)
-        if 0 <= t - 1 < BLOCKS:
-            pass_on(t - 1)
-        if t == 1:
-            for i in range(EARLY):
-                forward(1, i)
-        if 0 <= t - 2 < BLOCKS:
-            finish(t - 2)
-        pl.when(outer == 1)(functools.partial(move, t, OUTER, OUTER_TURNS))
-        pl.when(outer == 0)(functools.partial(move, t, INNER, INNER_TURNS))
+    def settle(b):
+        if b < BLOCKS:
+            finish(b)
+        pl.when(outer == 1)(functools.partial(move, b + 2, OUTER, OUTER_TURNS))
+        pl.when(outer == 0)(functools.partial(move, b + 2, INNER, INNER_TURNS))
+
+    got_a(0)
+    got_b(0, 0)
+    chunk(0, 0)
+    got_b(0, 1)
+    chunk(0, 1)
+    got_a(1)
+    chunk(1, 0)
+    chunk(1, 1)
+    got_b(0, 2)
+    chunk(0, 2)
+    chunk(1, 2)
+    pass_on(0)
+    got_b(0, 3)
+    chunk(0, 3)
+    chunk(1, 3)
+    pass_on(1)
+    for i in range(4):
+        got_b(1, i)
+        chunk(2, i)
+        chunk(3, i)
+        if i == 1:
+            settle(0)
+        if i == 2:
+            settle(1)
+            pass_on(2)
+    pass_on(3)
+    got_a(2)
+    begin(4)
+    settle(2)
+    got_a(3)
+    begin(5)
+    pass_on(4)
+    settle(3)
+    begin(6)
+    pass_on(5)
+    settle(4)
+    begin(7)
+    pass_on(6)
+    settle(5)
+    pass_on(7)
+    settle(6)
+    settle(7)
+    settle(8)
 
     for half in range(2):
         for d in range(2):
@@ -279,7 +320,8 @@
             b_forward(half, i, 2 + core).wait_send()
     for b in range(BLOCKS):
         for d in range(2):
-            near_copy(b, d).wait_send()
+            near_copy(b, d, 0).wait_send()
+            near_copy(b, d, 1).wait_send()
             far_copy(b, d).wait_send()
     for d in range(2):
         z_first_copy(d).wait_send()
@@ -309,7 +351,7 @@
             pltpu.VMEM((2, 2, ROWS, COLS), jnp.float32),
             pltpu.VMEM((ROWS, COLS), jnp.float32),
             dma((4, 2)), dma((4, 2)), dma((2,)), dma((2,)), dma((2,)), dma((2, 4)), dma((2, 4)), dma((2, 4)), dma((2, 4)),
-            dma((BLOCKS, 2)), dma((BLOCKS, 2)), dma((BLOCKS, 2)), dma((BLOCKS, 2)),
+            dma((BLOCKS, 2, 2)), dma((BLOCKS, 2, 2)), dma((BLOCKS, 2)), dma((BLOCKS, 2)),
             dma((2,)), dma((2,)), dma((2, 2)), dma((2, 2)), dma((2, 2)), dma((2, 2)), dma(()), dma(()),
         ],
         compiler_params=pltpu.CompilerParams(collective_id=0, has_side_effects=True, vmem_limit_bytes=60 << 20),

time: 65.4 us -> 61.2 us (0.936)
  Pallas kernels: 63.8 us -> 59.7 us
    pallas_call x1, Pallas kernels: 63.8 us -> 59.7 us  [local(): pl.pallas_call(kernel, out_shape=jax.ShapeDtypeStruct((ROWS, COLS), jnp.f...]
where the time goes in v3:
time: 61.2 us; the launch traced here: 61.1 us
  Pallas kernels  59.7 us (98%)
  other arithmetic  1.43 us (2%)
    pallas_call x1, Pallas kernels, local(): pl.pallas_call(kernel, out_shape=jax.ShapeDtypeStruct((ROWS, COLS), jnp.f...  59.7 us
    add x1, other arithmetic, local(): return residual_in + ladder  1.43 us

profile of v3, /device:TPU:32, one launch (start us, length us, event | category | flops | bytes accessed | tf_op | source)
XLA Modules:
  0.0 61.1 jit_solution(13943385284833917286)
XLA Ops:
  0.0 0.0 copy-start
  0.0 59.7 %ladder.1 = f32[48,256]{1,0:T(8,128)} custom-call(bf16[48,8192]{1,0:T(8,128)(2,1)} %a_ref.1, bf16[4,2,256,256]{3,2,1,0:T(8,128)(2,1)} %bitcast.1), custom_call_target="tpu_custom_call" | custom-call | tf_op jit(solution)/shard_map/ladder/pallas_call | solution.py:338
  59.7 0.0 copy-done
  59.7 1.4 %add.3 = f32[48,256]{1,0:T(8,128)} add(f32[48,256]{1,0:T(8,128)S(1)} %copy-done, f32[48,256]{1,0:T(8,128)} %ladder.1) | non-fusion elementwise | flops 12288 | bytes 147456 | tf_op jit(solution)/shard_map/add | solution.py:360
Async XLA Ops:
  0.0 59.7 %copy-start = (f32[48,256]{1,0:T(8,128)S(1)}, f32[48,256]{1,0:T(8,128)}, u32[]{:S(2)}) copy-start(f32[48,256]{1,0:T(8,128)} %param.5) | copy-start | bytes 147460

commit v4 on v3

--- a/solution.py
+++ b/solution.py
@@ -22,8 +22,8 @@
 OUTER_TURNS = (2, 4, 4, 10, 6, 8, 8, 9)
 INNER_TURNS = (2, 4, 4, 10, 6, 7, 8, 10)
 SCHEDULE = {
-    "init": [("b", 0, 0), ("m", 0), ("a", 2, 0), ("a", 0, 1), ("b", 0, 1), ("a", 2, 1), ("b", 0, 2), ("b", 0, 3), ("a", 0, 2), ("a", 0, 3)],
-    ("got", 0, 0): [("b", 1, 0), ("b", 1, 1), ("b", 1, 2), ("b", 1, 3)],
+    "init": [("b", 0, 0), ("m", 0), ("a", 2, 0), ("a", 0, 1), ("b", 0, 1), ("a", 2, 1), ("b", 0, 2), ("b", 0, 3), ("b", 1, 0), ("a", 0, 2), ("a", 0, 3)],
+    ("got", 0, 0): [("b", 1, 1), ("b", 1, 2), ("b", 1, 3)],
     ("got", 0, 3): [("m", 1), ("a", 2, 2)],
     ("got", 1, 0): [("a", 2, 3)],
 }
@@ -169,9 +169,9 @@
             device_id=device(x, y, z + 1 - 2 * d, core), device_id_type=MESH,
         )
 
-    def z_ring_copy(b, d, step):
-        return pltpu.make_async_remote_copy(
-            part.at[b, pl.ds(6, 2)], z_ring.at[step, d], zr_send.at[step, d], zr_recv.at[step, d],
+    def z_ring_copy(b, d, step, half):
+        return pltpu.make_async_remote_copy(
+            part.at[b, 6 + half], z_ring.at[step, d, half], zr_send.at[step, d, half], zr_recv.at[step, d, half],
             device_id=device(x, y, z + 1 - 2 * d, core), device_id_type=MESH,
         )
 
@@ -234,17 +234,18 @@
             z_first_copy(0).start()
             z_first_copy(1).start()
         elif abs(step) == 3:
+            z_ring_copy(b, d, 0, 1 - d).start()
             z_first_copy(d).wait_recv()
             part[b, 6 + d] += z_first[d]
-            z_ring_copy(b, d, 0).start()
+            z_ring_copy(b, d, 0, d).start()
         elif step:
-            z_ring_copy(b, d, 2 - abs(step)).wait_recv()
-            part[b, pl.ds(6, 2)] += z_ring[2 - abs(step), d]
-            if abs(step) == 2:
-                z_ring_copy(b, d, 1).start()
-            else:
-                z_last_copy(b, d, 1).start()
-                z_last_copy(b, d, 0).start()
+            for half in (1, 0):
+                z_ring_copy(b, d, 2 - abs(step), half).wait_recv()
+                part[b, 6 + half] += z_ring[2 - abs(step), d, half]
+                if abs(step) == 2:
+                    z_ring_copy(b, d, 1, half).start()
+                else:
+                    z_last_copy(b, d, half).start()
         else:
             x_last_copy.start()
 
@@ -287,15 +288,15 @@
     pass_on(3)
     got_a(2)
     begin(4)
-    settle(2)
     got_a(3)
     begin(5)
+    settle(2)
     pass_on(4)
+    begin(6)
     settle(3)
-    begin(6)
     pass_on(5)
+    begin(7)
     settle(4)
-    begin(7)
     pass_on(6)
     settle(5)
     pass_on(7)
@@ -326,7 +327,8 @@
     for d in range(2):
         z_first_copy(d).wait_send()
         for step in range(2):
-            z_ring_copy(1, d, step).wait_send()
+            for half in range(2):
+                z_ring_copy(1, d, step, half).wait_send()
         for half in range(2):
             z_last_copy(5, d, half).wait_send()
     x_last_copy.wait_send()
@@ -352,7 +354,7 @@
             pltpu.VMEM((ROWS, COLS), jnp.float32),
             dma((4, 2)), dma((4, 2)), dma((2,)), dma((2,)), dma((2,)), dma((2, 4)), dma((2, 4)), dma((2, 4)), dma((2, 4)),
             dma((BLOCKS, 2, 2)), dma((BLOCKS, 2, 2)), dma((BLOCKS, 2)), dma((BLOCKS, 2)),
-            dma((2,)), dma((2,)), dma((2, 2)), dma((2, 2)), dma((2, 2)), dma((2, 2)), dma(()), dma(()),
+            dma((2,)), dma((2,)), dma((2, 2, 2)), dma((2, 2, 2)), dma((2, 2)), dma((2, 2)), dma(()), dma(()),
         ],
         compiler_params=pltpu.CompilerParams(collective_id=0, has_side_effects=True, vmem_limit_bytes=60 << 20),
         name="ladder",

time: 61.2 us -> 59.1 us (0.966)
  Pallas kernels: 59.7 us -> 57.6 us
    pallas_call x1, Pallas kernels: 59.7 us -> 57.6 us  [local(): pl.pallas_call(kernel, out_shape=jax.ShapeDtypeStruct((ROWS, COLS), jnp.f...]
where the time goes in v4:
time: 59.1 us; the launch traced here: 59 us
  Pallas kernels  57.6 us (97%)
  other arithmetic  1.43 us (2%)
    pallas_call x1, Pallas kernels, local(): pl.pallas_call(kernel, out_shape=jax.ShapeDtypeStruct((ROWS, COLS), jnp.f...  57.6 us
    add x1, other arithmetic, local(): return residual_in + ladder  1.43 us

profile of v4, /device:TPU:32, one launch (start us, length us, event | category | flops | bytes accessed | tf_op | source)
XLA Modules:
  0.0 59.0 jit_solution(5731899365572352462)
XLA Ops:
  0.0 0.0 copy-start
  0.0 57.6 %ladder.1 = f32[48,256]{1,0:T(8,128)} custom-call(bf16[48,8192]{1,0:T(8,128)(2,1)} %a_ref.1, bf16[4,2,256,256]{3,2,1,0:T(8,128)(2,1)} %bitcast.1), custom_call_target="tpu_custom_call" | custom-call | tf_op jit(solution)/shard_map/ladder/pallas_call | solution.py:340
  57.6 0.0 copy-done
  57.6 1.4 %add.3 = f32[48,256]{1,0:T(8,128)} add(f32[48,256]{1,0:T(8,128)S(1)} %copy-done, f32[48,256]{1,0:T(8,128)} %ladder.1) | non-fusion elementwise | flops 12288 | bytes 147456 | tf_op jit(solution)/shard_map/add | solution.py:362
Async XLA Ops:
  0.0 57.6 %copy-start = (f32[48,256]{1,0:T(8,128)S(1)}, f32[48,256]{1,0:T(8,128)}, u32[]{:S(2)}) copy-start(f32[48,256]{1,0:T(8,128)} %param.5) | copy-start | bytes 147460

commit v5 on v4

--- a/solution.py
+++ b/solution.py
@@ -19,8 +19,8 @@
 
 OUTER = (4, 3, 0, -1, -3, 2, -2, 1)
 INNER = (4, 3, 0, -1, -3, -2, 2, 1)
-OUTER_TURNS = (2, 4, 4, 10, 6, 8, 8, 9)
-INNER_TURNS = (2, 4, 4, 10, 6, 7, 8, 10)
+OUTER_TURNS = (2, 4, 4, 8, 6, 7, 8, 9)
+INNER_TURNS = (2, 4, 4, 9, 6, 7, 8, 9)
 SCHEDULE = {
     "init": [("b", 0, 0), ("m", 0), ("a", 2, 0), ("a", 0, 1), ("b", 0, 1), ("a", 2, 1), ("b", 0, 2), ("b", 0, 3), ("b", 1, 0), ("a", 0, 2), ("a", 0, 3)],
     ("got", 0, 0): [("b", 1, 1), ("b", 1, 2), ("b", 1, 3)],
@@ -192,11 +192,26 @@
 
     def chunk(b, i):
         multiply(b, i)
+        send(b, i)
+
+    def send(b, i):
         if i == 0:
             near_copy(b, 0, 0).start()
             near_copy(b, 1, 0).start()
         elif i < 3:
             near_copy(b, i - 1, 1).start()
+
+    def chunk2(b, c, i):
+        to = lax.rem(z + steps[b] + 8, 8)
+        other = lax.rem(z + steps[c] + 8, 8)
+        both = jnp.concatenate([a_all[lax.rem(to, 4)], a_all[lax.rem(other, 4)]], axis=0)
+        product = lax.dot_general(
+            both, b_all[lax.div(to, 4), lax.rem(y + OFFSETS[i], 4)], (((1,), (1,)), ((), ())), preferred_element_type=jnp.float32
+        )
+        for place, block in enumerate((b, c)):
+            part[block, TOP[i]] = product[2 * place * ROWS : (2 * place + 1) * ROWS]
+            part[block, BOTTOM[i]] = product[(2 * place + 1) * ROWS : (2 * place + 2) * ROWS]
+            send(block, i)
 
     def got_a(turn):
         if turn:
@@ -278,8 +293,7 @@
     pass_on(1)
     for i in range(4):
         got_b(1, i)
-        chunk(2, i)
-        chunk(3, i)
+        chunk2(2, 3, i)
         if i == 1:
             settle(0)
         if i == 2:
@@ -302,7 +316,6 @@
     pass_on(7)
     settle(6)
     settle(7)
-    settle(8)
 
     for half in range(2):
         for d in range(2):

time: 59.1 us -> 58.4 us (0.988)
  Pallas kernels: 57.6 us -> 56.9 us
    pallas_call x1, Pallas kernels: 57.6 us -> 56.9 us  [local(): pl.pallas_call(kernel, out_shape=jax.ShapeDtypeStruct((ROWS, COLS), jnp.f...]
where the time goes in v5:
time: 58.4 us; the launch traced here: 58.3 us
  Pallas kernels  56.9 us (97%)
  other arithmetic  1.43 us (2%)
    pallas_call x1, Pallas kernels, local(): pl.pallas_call(kernel, out_shape=jax.ShapeDtypeStruct((ROWS, COLS), jnp.f...  56.9 us
    add x1, other arithmetic, local(): return residual_in + ladder  1.43 us

profile of v5, /device:TPU:32, one launch (start us, length us, event | category | flops | bytes accessed | tf_op | source)
XLA Modules:
  0.0 58.3 jit_solution(3004594890635379575)
XLA Ops:
  0.0 0.0 copy-start
  0.0 56.9 %ladder.1 = f32[48,256]{1,0:T(8,128)} custom-call(bf16[48,8192]{1,0:T(8,128)(2,1)} %a_ref.1, bf16[4,2,256,256]{3,2,1,0:T(8,128)(2,1)} %bitcast.1), custom_call_target="tpu_custom_call" | custom-call | tf_op jit(solution)/shard_map/ladder/pallas_call | solution.py:353
  56.9 0.0 copy-done
  56.9 1.4 %add.3 = f32[48,256]{1,0:T(8,128)} add(f32[48,256]{1,0:T(8,128)S(1)} %copy-done, f32[48,256]{1,0:T(8,128)} %ladder.1) | non-fusion elementwise | flops 12288 | bytes 147456 | tf_op jit(solution)/shard_map/add | solution.py:375
Async XLA Ops:
  0.0 56.9 %copy-start = (f32[48,256]{1,0:T(8,128)S(1)}, f32[48,256]{1,0:T(8,128)}, u32[]{:S(2)}) copy-start(f32[48,256]{1,0:T(8,128)} %param.5) | copy-start | bytes 147460
